TPU v7x, 32 devices: a whole 2x2x4 slice. The times are simulated.
32 devices in a mesh: dm: 4 (over z), hv: 8 (over y, x, core).
Axes of the slice: x: 2, y: 2, z: 4, core: 2. Of those that a mesh axis runs over, the one named last changes fastest.
Arguments:
- tokens: bfloat16 [512, 16384], P('hv', 'dm'), may hold values from -64 to 64
- gate_weight: bfloat16 [16384, 13312], P('dm', 'hv'), may hold values from -0.046875 to 0.046875
- up_weight: bfloat16 [16384, 13312], P('dm', 'hv'), may hold values from -0.046875 to 0.046875
- down_weight: bfloat16 [13312, 16384], P('hv', 'dm'), may hold values from -0.0546875 to 0.0546875
- norm_gain: float32 [16384], P('dm'), may hold values from 0.1 to 1.9
- unembed: bfloat16 [16384, 32064], P('dm', 'hv'), may hold values from -8 to 8
- gold_ids: int32 [512], replicated, may hold values from 0 to 32063
- option_lengths: int32 [32], replicated, may hold values from 1 to 32, 512 in all
Outputs:
- token_logprob: float32 [512], replicated
- option_score: float32 [32], replicated
All inputs are finite; a program needn't handle non-finite values.
Results may differ from a plain program's by a relative error of at most 0.005.
Values may be sent and summed in bfloat16 or wider, within the bound.
No kernel may reach another device: no remote copies, remote signals or barrier semaphores. Data moves between devices by JAX's collectives and lax.ppermute only.
A program may use at most 128 MiB of HBM per device.

v0:
```python
import jax
import jax.numpy as jnp
from jax import lax
from jax.sharding import PartitionSpec as P

D = 16384


def row_logprob(logits, golds, offset):
    hit = lax.broadcasted_iota(jnp.int32, logits.shape, 1) + offset == golds[:, None]
    gold_part = jnp.sum(jnp.where(hit, logits, 0.0), axis=1)
    top = lax.pmax(jnp.max(logits, axis=1), "hv")
    local_total = jnp.sum(jnp.exp(logits - top[:, None]), axis=1)
    total, gold = lax.psum((local_total, gold_part), "hv")
    return gold - top - jnp.log(total)


def per_device(
    tokens, gate_weight, up_weight, down_weight, norm_gain, unembed, gold_ids, option_lengths
):
    width = gate_weight.shape[1]
    piece = lax.all_gather(tokens, "hv", axis=0, tiled=True)
    gate = jnp.dot(piece, gate_weight, preferred_element_type=jnp.float32)
    up = jnp.dot(piece, up_weight, preferred_element_type=jnp.float32)
    partial_in = jnp.concatenate([gate, up], axis=1)
    summed = lax.psum(partial_in, "dm")
    hidden = (jax.nn.silu(summed[:, :width]) * summed[:, width:]).astype(jnp.bfloat16)
    ffn = lax.psum_scatter(
        jnp.dot(hidden, down_weight, preferred_element_type=jnp.float32),
        "hv",
        scatter_dimension=0,
        tiled=True,
    )
    resid = (tokens.astype(jnp.float32) + ffn).astype(jnp.bfloat16)
    wide = resid.astype(jnp.float32)
    squares = lax.psum(jnp.sum(wide * wide, axis=1), "dm")
    normed = (wide * lax.rsqrt(squares[:, None] / D + 1e-05) * norm_gain).astype(jnp.bfloat16)
    partial_logits = jnp.dot(
        lax.all_gather(normed, "hv", axis=0, tiled=True),
        unembed,
        preferred_element_type=jnp.float32,
    )
    offset = lax.axis_index("hv") * unembed.shape[1]
    logits = lax.psum(partial_logits, "dm")
    token_logprob = row_logprob(logits, gold_ids, offset)
    ends = jnp.cumsum(option_lengths)
    starts = ends - option_lengths
    places = jnp.arange(token_logprob.shape[0], dtype=jnp.int32)
    member = ((places[None, :] >= starts[:, None]) & (places[None, :] < ends[:, None])).astype(
        jnp.float32
    )
    option_sums = jnp.dot(member, token_logprob, precision=lax.Precision.HIGHEST)
    option_score = option_sums / option_lengths.astype(jnp.float32)
    return (token_logprob, option_score)


def solution(mesh):
    placed = (
        P("hv", "dm"),
        P("dm", "hv"),
        P("dm", "hv"),
        P("hv", "dm"),
        P("dm"),
        P("dm", "hv"),
        P(),
        P(),
    )
    return jax.shard_map(
        per_device, mesh=mesh, in_specs=placed, out_specs=(P(), P()), check_vma=False
    )
```

profile of v0, /device:TPU:0, one launch (start us, length us, event | category | flops | bytes accessed | tf_op | source)
XLA Modules:
  0.0 802.2 jit_solution(8967663824214482826)
XLA Ops:
  7.2 0.7 all-gather.3.cloned.1.call-update
  7.9 41.4 %all-gather.3.cloned.1.call-done = bf16[512,4096]{1,0:T(8,128)(2,1)} async-done(((bf16[64,4096]{1,0:T(8,128)(2,1)}), bf16[512,4096]{1,0:T(8,128)(2,1)}) %all-gather.3.cloned.1.call-update) | async-done | bytes 4194320 | tf_op jit(solution)/shard_map/all_gather | solution.py:22
  49.3 11.7 %fusion.13 = f32[512,1664]{1,0:T(8,128)S(1)} fusion(bf16[512,4096]{1,0:T(8,128)(2,1)} %all-gather.3.cloned.1.call-done, bf16[4096,1664]{1,0:T(8,128)(2,1)} %param.9), kind=kOutput, calls=%fused_computation.24 | convolution fusion | flops 6979321856 | bytes 21233664 | tf_op jit(solution)/shard_map/dot_general | solution.py:23
  61.0 11.0 %fusion.14 = f32[512,1664]{1,0:T(8,128)S(1)} fusion(bf16[512,4096]{1,0:T(8,128)(2,1)S(1)} %copy-done.5, bf16[4096,1664]{1,0:T(8,128)(2,1)} %param.10), kind=kOutput, calls=%fused_computation.25 | convolution fusion | flops 6979321856 | bytes 21233664 | tf_op jit(solution)/shard_map/dot_general | solution.py:24
  72.0 3.3 pad_maximum_fusion
  75.4 239.9 %all-reduce.4.cloned.1.call-done = f32[512,3328]{1,0:T(8,128)} async-done(((f32[512,3328]{1,0:T(8,128)}), f32[512,3328]{1,0:T(8,128)}) %all-reduce.4.cloned.1.call-update) | async-done | bytes 6815760 | tf_op jit(solution)/shard_map/psum | solution.py:26
  315.3 15.9 %fusion.1 = f32[512,4096]{1,0:T(8,128)} fusion(bf16[1664,4096]{1,0:T(8,128)(2,1)} %param.11, f32[512,3328]{1,0:T(8,128)} %all-reduce.4.cloned.1.call-done), kind=kOutput, calls=%fused_computation.5 | convolution fusion | flops 6984433664 | bytes 28835840 | tf_op jit(solution)/shard_map/dot_general | solution.py:29
  331.3 70.3 %reduce-scatter.2.cloned.1.call-done = f32[64,4096]{1,0:T(8,128)} async-done(((f32[512,4096]{1,0:T(8,128)}), f32[64,4096]{1,0:T(8,128)}) %reduce-scatter.2.cloned.1.call-update) | async-done | bytes 1048592 | tf_op jit(solution)/shard_map/reduce_scatter | solution.py:28
  401.6 1.5 fusion.5
  403.0 11.7 %psum.36 = f32[64]{0:T(128)S(1)} all-reduce(f32[64]{0:T(128)S(1)} %fusion.5), channel_id=1, replica_groups=mesh['dm'=4,'hv'=8] {'dm'}, use_global_device_ids=true, to_apply=%region_3.4 | all-reduce | flops 64 | bytes 512 | tf_op jit(solution)/shard_map/psum | solution.py:36
  414.8 2.2 fusion.7
  417.0 0.2 all-reduce.6.cloned.1.call-start
  417.2 33.8 %all-gather.5.cloned.1.call-done = bf16[512,4096]{1,0:T(8,128)(2,1)} async-done(((bf16[64,4096]{1,0:T(8,128)(2,1)}), bf16[512,4096]{1,0:T(8,128)(2,1)}) %all-gather.5.cloned.1.call-update) | async-done | bytes 4194320 | tf_op jit(solution)/shard_map/all_gather | solution.py:39
  451.0 23.7 %fusion.15 = f32[512,4008]{0,1:T(8,128)} fusion(bf16[512,4096]{1,0:T(8,128)(2,1)} %all-gather.5.cloned.1.call-done, bf16[4096,4008]{0,1:T(8,128)(2,1)} %param.13), kind=kOutput, calls=%fused_computation.26 | convolution fusion | flops 16810770432 | bytes 45236224 | tf_op jit(solution)/shard_map/dot_general | solution.py:38
  474.8 0.6 copy-done.4
  475.4 0.1 copy.11
  475.5 0.1 reduce-window.8
  475.5 0.1 reduce
  475.7 284.8 %all-reduce.6.cloned.1.call-done = f32[512,4008]{0,1:T(8,128)} async-done(((f32[512,4008]{0,1:T(8,128)}), f32[512,4008]{0,1:T(8,128)}) %all-reduce.6.cloned.1.call-update) | async-done | bytes 8208400 | tf_op jit(solution)/shard_map/psum | solution.py:44
  760.5 3.9 reduce_max.9
  764.4 13.6 %pmax.7 = f32[512]{0:T(512)S(1)} all-reduce(f32[512]{0:T(512)S(1)} %reduce_max.9), channel_id=1, replica_groups=mesh['dm'=4,'hv'=8] {'hv'}, use_global_device_ids=true, to_apply=%region_8.9 | all-reduce | flops 512 | bytes 4096 | tf_op jit(solution)/shard_map/pmax | solution.py:12
  778.0 5.1 select_reduce_fusion
  783.1 11.8 %all-reduce = (f32[512]{0:T(512)S(1)}, f32[512]{0:T(512)S(1)}) all-reduce(f32[512]{0:T(512)S(1)} %get-tuple-element.3, f32[512]{0:T(512)S(1)} %get-tuple-element.2), channel_id=1, replica_groups=mesh['dm'=4,'hv'=8] {'hv'}, use_global_device_ids=true, to_apply=%region_10.11 | all-reduce | flops 1024 | bytes 8192 | tf_op jit(solution)/shard_map/psum | solution.py:14
  794.9 0.7 fusion.4
  (23 shorter events, 0.3 us)
Async XLA Ops:
  7.2 42.2 %all-gather.3.cloned.1.call-start = ((), (), s32[]{:S(2)}) async-start(), calls=%async_computation.1 | async-start | bytes 4718592 | tf_op jit(solution)/shard_map/all_gather | solution.py:22
  7.9 307.4 %all-reduce.4.cloned.1.call-start = ((), (), s32[]{:S(2)}) async-start(), calls=%async_computation.2 | async-start | bytes 13631488 | tf_op jit(solution)/shard_map/psum | solution.py:26
  49.3 11.7 %copy-start.5 = (bf16[512,4096]{1,0:T(8,128)(2,1)S(1)}, bf16[512,4096]{1,0:T(8,128)(2,1)}, u32[]{:S(2)}) copy-start(bf16[512,4096]{1,0:T(8,128)(2,1)} %all-gather.3.cloned.1.call-done) | copy-start | bytes 12582916
  75.3 326.2 %reduce-scatter.2.cloned.1.call-start = ((), (), s32[]{:S(2)}) async-start(), calls=%async_computation.3 | async-start | bytes 9437184 | tf_op jit(solution)/shard_map/reduce_scatter | solution.py:28
  331.2 70.4 %copy-start = (bf16[64,4096]{1,0:T(8,128)(2,1)S(1)}, bf16[64,4096]{1,0:T(8,128)(2,1)}, u32[]{:S(2)}) copy-start(bf16[64,4096]{1,0:T(8,128)(2,1)} %param.8) | copy-start | bytes 1572868
  331.2 83.6 %copy-start.1 = (f32[4096]{0:T(1024)S(1)}, f32[4096]{0:T(1024)}, u32[]{:S(2)}) copy-start(f32[4096]{0:T(1024)} %param.12) | copy-start | bytes 49156
  331.2 119.8 %all-gather.5.cloned.1.call-start = ((), (), s32[]{:S(2)}) async-start(), calls=%async_computation.4 | async-start | bytes 4718592 | tf_op jit(solution)/shard_map/all_gather | solution.py:39
  417.0 343.5 %all-reduce.6.cloned.1.call-start = ((), (), s32[]{:S(2)}) async-start(), calls=%async_computation.5 | async-start | bytes 16416768 | tf_op jit(solution)/shard_map/psum | solution.py:44
  474.7 0.7 copy-start.4
  474.8 303.3 %copy-start.2 = (s32[512]{0:T(512)S(1)}, s32[512]{0:T(512)}, u32[]{:S(2)}) copy-start(s32[512]{0:T(512)} %param.14) | copy-start | bytes 6148
  794.9 0.7 copy-start.3
Sparse Core Ops, SparseCore 0:
  9.9 39.4 all-gather.2
  75.4 239.7 all-reduce.3
  331.3 70.1 reduce-scatter.1
  417.1 33.9 all-gather.4
  474.9 285.5 all-reduce.5
where the time goes:
time: 803 us; the launch traced here: 802 us
  waiting for transfers between devices  671 us (84%)
  matrix products  63 us (8%)
  blocking collectives  37.1 us (5%)
  other arithmetic  16.1 us (2%)
  between operations  13.8 us (2%)
    psum x1, waiting for transfers between devices, per_device(): logits = lax.psum(partial_logits, 'dm')  285 us
    psum x1, waiting for transfers between devices, per_device(): summed = lax.psum(partial_in, 'dm')  240 us
    reduce_scatter x1, waiting for transfers between devices, per_device(): lax.psum_scatter(jnp.dot(hidden, down_weight, preferred_element_type=jnp....  70.3 us
    all_gather x1, waiting for transfers between devices, per_device(): piece = lax.all_gather(tokens, 'hv', axis=0, tiled=True)  41.4 us
    all_gather x1, waiting for transfers between devices, per_device(): lax.all_gather(normed, 'hv', axis=0, tiled=True)  33.8 us
    dot_general x1, matrix products, per_device(): jnp.dot(lax.all_gather(normed, 'hv', axis=0, tiled=True), unembed, prefer...  23.7 us
  transfers between devices with their start and end apart: 5, of which 5 were waited for; matrix products, arithmetic and copies ran while one was open for 0% of the time, Pallas kernels for 0%

commit v1 on v0

v1 whole, which is shorter than its diff:
```python
import functools

import jax
import jax.numpy as jnp
import numpy as np
from jax import lax
from jax.sharding import PartitionSpec as P

D = 16384
BATCHES = 2
F32 = jnp.float32
BF16 = jnp.bfloat16


def dm_steps(n):
    return [(lambda i, k=k: (i >> k) & 1, lambda i, k=k: i ^ (1 << k)) for k in range(n.bit_length() - 1)]


def hv_steps(n):
    if n != 8:
        return dm_steps(n)
    return [
        (lambda i: i & 1, lambda i: i ^ 1),
        (lambda i: (i >> (1 + (i & 1))) & 1, lambda i: i ^ (2 << (i & 1))),
        (lambda i: (i >> (2 - (i & 1))) & 1, lambda i: i ^ (4 >> (i & 1))),
    ]


def places(steps, n):
    out = []
    for i in range(n):
        place = 0
        for bit, _ in steps:
            place = 2 * place + bit(i)
        out.append(place)
    return np.array(out)


def scatter(array, axis, steps, n):
    index = lax.axis_index(axis)
    for bit, partner in steps:
        half = array.shape[0] // 2
        mine = bit(index)
        sent = lax.dynamic_slice_in_dim(array, (1 - mine) * half, half, 0)
        got = lax.ppermute(sent, axis, [(i, partner(i)) for i in range(n)])
        kept = lax.dynamic_slice_in_dim(array, mine * half, half, 0)
        array = (kept.astype(F32) + got.astype(F32)).astype(BF16)
    return array


def gather(array, axis, steps, n):
    index = lax.axis_index(axis)
    for bit, partner in reversed(steps):
        got = lax.ppermute(array, axis, [(i, partner(i)) for i in range(n)])
        low = bit(index) == 0
        array = jnp.concatenate([jnp.where(low, array, got), jnp.where(low, got, array)], axis=0)
    return array


def per_device(
    tokens, gate_weight, up_weight, down_weight, norm_gain, unembed, gold_ids, option_lengths, *, n_dm, n_hv
):
    width = gate_weight.shape[1]
    own = tokens.shape[0] // BATCHES
    rows = own * n_hv
    over_dm, over_hv = dm_steps(n_dm), hv_steps(n_hv)
    dm_place, hv_place = places(over_dm, n_dm), places(over_hv, n_hv)
    dm, hv = lax.axis_index("dm"), lax.axis_index("hv")
    spot = jnp.asarray(dm_place)[dm]
    share = rows // n_dm
    golds = gold_ids.reshape(n_hv, BATCHES, own)[np.argsort(hv_place)]
    offset = hv * unembed.shape[1]
    stats = []
    for b in range(BATCHES):
        mine = tokens[b * own : (b + 1) * own]
        piece = gather(mine, "hv", over_hv, n_hv)
        gate = jnp.dot(piece, gate_weight, preferred_element_type=F32).astype(BF16)
        up = jnp.dot(piece, up_weight, preferred_element_type=F32).astype(BF16)
        summed = scatter(jnp.concatenate([gate, up], axis=1), "dm", over_dm, n_dm).astype(F32)
        hidden = (jax.nn.silu(summed[:, :width]) * summed[:, width:]).astype(BF16)
        hidden = gather(hidden, "dm", over_dm, n_dm)
        ffn = jnp.dot(hidden, down_weight, preferred_element_type=F32).astype(BF16)
        ffn = scatter(ffn, "hv", over_hv, n_hv)
        resid = (mine.astype(F32) + ffn.astype(F32)).astype(BF16)
        whole = gather(resid, "hv", over_hv, n_hv)
        wide = whole.astype(F32)
        squares = lax.psum(jnp.sum(wide * wide, axis=1), "dm")
        scaled = (wide * norm_gain).astype(BF16)
        partial = jnp.dot(scaled, unembed, preferred_element_type=F32).astype(BF16)
        part = scatter(partial, "dm", over_dm, n_dm)
        scale = lax.rsqrt(lax.dynamic_slice_in_dim(squares, spot * share, share, 0) / D + 1e-05)
        logits = part.astype(F32) * scale[:, None]
        gold = lax.dynamic_slice_in_dim(golds[:, b].reshape(-1), spot * share, share, 0)
        hit = lax.broadcasted_iota(jnp.int32, logits.shape, 1) + offset == gold[:, None]
        gold_part = jnp.sum(jnp.where(hit, logits, 0.0), axis=1)
        top = jnp.max(logits, axis=1)
        total = jnp.sum(jnp.exp(logits - top[:, None]), axis=1)
        stats.append(jnp.stack([top, total, gold_part]))
    stats = lax.all_gather(jnp.stack(stats), "hv", axis=0)
    top = jnp.max(stats[:, :, 0], axis=0)
    total = jnp.sum(stats[:, :, 1] * jnp.exp(stats[:, :, 0] - top), axis=0)
    gold = jnp.sum(stats[:, :, 2], axis=0)
    logprob = lax.all_gather(gold - top - jnp.log(total), "dm", axis=0)
    logprob = logprob[np.argsort(dm_place)]
    logprob = logprob.transpose(1, 0, 2).reshape(BATCHES, n_hv, own)
    token_logprob = logprob[:, hv_place].transpose(1, 0, 2).reshape(-1)
    ends = jnp.cumsum(option_lengths)
    starts = ends - option_lengths
    spots = jnp.arange(token_logprob.shape[0], dtype=jnp.int32)
    member = ((spots[None, :] >= starts[:, None]) & (spots[None, :] < ends[:, None])).astype(F32)
    option_sums = jnp.dot(member, token_logprob, precision=lax.Precision.HIGHEST)
    option_score = option_sums / option_lengths.astype(F32)
    return (token_logprob, option_score)


def solution(mesh):
    placed = (
        P("hv", "dm"),
        P("dm", "hv"),
        P("dm", "hv"),
        P("hv", "dm"),
        P("dm"),
        P("dm", "hv"),
        P(),
        P(),
    )
    body = functools.partial(per_device, n_dm=mesh.shape["dm"], n_hv=mesh.shape["hv"])
    return jax.shard_map(
        body, mesh=mesh, in_specs=placed, out_specs=(P(), P()), check_vma=False
    )
```

time: 803 us -> 339 us (0.42)
  waiting for transfers between devices: 671 us -> 165 us
  starting transfers between devices: 0.38 us -> 37.3 us
  local copies, waits for them, and re-layouts: 0.73 us -> 15.7 us
  between operations: 13.8 us -> 2.06 us
    psum x2 -> x0, waiting for transfers between devices: 525 us -> none  [the longest x1 285 us: per_device(): logits = lax.psum(partial_logits, 'dm')]
    ppermute x0 -> x30, waiting for transfers between devices: none -> 165 us  [the longest x14 96.1 us: scatter(): got = lax.ppermute(sent, axis, [(i, partner(i)) for i in range(n)])]
    all_gather x2 -> x0, waiting for transfers between devices: 75.2 us -> none  [the longest x1 41.4 us: per_device(): piece = lax.all_gather(tokens, 'hv', axis=0, tiled=True)]
    reduce_scatter x1 -> x0, waiting for transfers between devices: 70.3 us -> none  [per_device(): lax.psum_scatter(jnp.dot(hidden, down_weight, preferred_element_type=jnp....]
    ppermute x0 -> x30, starting transfers between devices: none -> 37.3 us  [the longest x16 20.7 us: gather(): got = lax.ppermute(array, axis, [(i, partner(i)) for i in range(n)])]
    all_gather x0 -> x2, blocking collectives: none -> 25.2 us  [the longest x1 16.3 us: per_device(): logprob = lax.all_gather(gold - top - jnp.log(total), 'dm', axis=0)]
    pmax x1 -> x0, blocking collectives: 13.6 us -> none  [row_logprob(): top = lax.pmax(jnp.max(logits, axis=1), 'hv')]
    psum x1 -> x0, blocking collectives: 11.8 us -> none  [row_logprob(): total, gold = lax.psum((local_total, gold_part), 'hv')]
  transfers between devices with their start and end apart: 5 -> 30, of which waited for: 5 -> 21; matrix products, arithmetic and copies ran while one was open for 0% -> 24% of each run, Pallas kernels for 0% -> 0%
where the time goes in v1:
time: 339 us; the launch traced here: 338 us
  waiting for transfers between devices  165 us (49%)
  matrix products  60.9 us (18%)
  blocking collectives  41 us (12%)
  starting transfers between devices  37.3 us (11%)
  other arithmetic  16.4 us (5%)
  local copies, waits for them, and re-layouts  15.7 us (5%)
    ppermute x14, waiting for transfers between devices, scatter(): got = lax.ppermute(sent, axis, [(i, partner(i)) for i in range(n)])  96.1 us
    ppermute x16, waiting for transfers between devices, gather(): got = lax.ppermute(array, axis, [(i, partner(i)) for i in range(n)])  68.6 us
    dot_general x2, matrix products, per_device(): partial = jnp.dot(scaled, unembed, preferred_element_type=F32).astype(BF16)  28.9 us
    ppermute x16, starting transfers between devices, gather(): got = lax.ppermute(array, axis, [(i, partner(i)) for i in range(n)])  20.7 us
    ppermute x14, starting transfers between devices, scatter(): got = lax.ppermute(sent, axis, [(i, partner(i)) for i in range(n)])  16.6 us
    all_gather x1, blocking collectives, per_device(): logprob = lax.all_gather(gold - top - jnp.log(total), 'dm', axis=0)  16.3 us
    psum x1, blocking collectives, per_device(): squares = lax.psum(jnp.sum(wide * wide, axis=1), 'dm')  15.8 us
    dot_general x2, matrix products, per_device(): up = jnp.dot(piece, up_weight, preferred_element_type=F32).astype(BF16)  14.8 us
  transfers between devices with their start and end apart: 30, of which 21 were waited for; matrix products, arithmetic and copies ran while one was open for 24% of the time, Pallas kernels for 0%

profile of v1, /device:TPU:0, one launch (start us, length us, event | category | flops | bytes accessed | tf_op | source)
XLA Modules:
  0.0 338.0 jit_solution(17571231917738445689)
XLA Ops:
  4.7 4.4 %collective-permute-done = bf16[32,4096]{1,0:T(8,128)(2,1)S(1)} collective-permute-done((bf16[32,4096]{1,0:T(8,128)(2,1)S(1)}, bf16[32,4096]{1,0:T(8,128)(2,1)S(1)}, u32[]{:S(2)}, u32[]{:S(2)}) %collective-permute-start) | collective-permute-done | bytes 262176 | tf_op jit(solution)/shard_map/ppermute | solution.py:54
  13.8 5.6 %collective-permute-done.15 = bf16[32,4096]{1,0:T(8,128)(2,1)S(1)} collective-permute-done((bf16[32,4096]{1,0:T(8,128)(2,1)S(1)}, bf16[32,4096]{1,0:T(8,128)(2,1)S(1)}, u32[]{:S(2)}, u32[]{:S(2)}) %collective-permute-start.15) | collective-permute-done | bytes 262176 | tf_op jit(solution)/shard_map/ppermute | solution.py:54
  22.2 6.6 %collective-permute-done.16 = bf16[64,4096]{1,0:T(8,128)(2,1)S(1)} collective-permute-done((bf16[64,4096]{1,0:T(8,128)(2,1)S(1)}, bf16[64,4096]{1,0:T(8,128)(2,1)S(1)}, u32[]{:S(2)}, u32[]{:S(2)}) %collective-permute-start.16) | collective-permute-done | bytes 524320 | tf_op jit(solution)/shard_map/ppermute | solution.py:54
  33.6 7.4 %convolution_convert_fusion.6 = bf16[256,1664]{1,0:T(8,128)(2,1)S(1)} fusion(bf16[4096,1664]{1,0:T(8,128)(2,1)} %param.17, bf16[128,4096]{1,0:T(8,128)(2,1)S(1)} %get-tuple-element.17, bf16[128,4096]{1,0:T(8,128)(2,1)S(1)} %get-tuple-element.16), kind=kOutput, calls=%fused_computation.17 | convolution fusion | flops 3494281216 | bytes 16580608 | tf_op jit(solution)/shard_map/dot_general | solution.py:78
  47.6 7.4 %convolution_convert_fusion.4 = bf16[256,1664]{1,0:T(8,128)(2,1)S(1)} fusion(bf16[4096,1664]{1,0:T(8,128)(2,1)} %param.17, bf16[128,4096]{1,0:T(8,128)(2,1)S(1)} %get-tuple-element.21, bf16[128,4096]{1,0:T(8,128)(2,1)S(1)} %get-tuple-element.20), kind=kOutput, calls=%fused_computation.15 | convolution fusion | flops 3494281216 | bytes 16580608 | tf_op jit(solution)/shard_map/dot_general | solution.py:78
  55.2 7.8 %collective-permute-done.3 = bf16[128,3328]{1,0:T(8,128)(2,1)S(1)} collective-permute-done((bf16[128,3328]{1,0:T(8,128)(2,1)S(1)}, bf16[128,3328]{1,0:T(8,128)(2,1)S(1)}, u32[]{:S(2)}, u32[]{:S(2)}) %collective-permute-start.3) | collective-permute-done | bytes 852000 | tf_op jit(solution)/shard_map/ppermute | solution.py:45
  66.2 23.9 %collective-permute-done.18 = bf16[128,3328]{1,0:T(8,128)(2,1)S(1)} collective-permute-done((bf16[128,3328]{1,0:T(8,128)(2,1)S(1)}, bf16[128,3328]{1,0:T(8,128)(2,1)S(1)}, u32[]{:S(2)}, u32[]{:S(2)}) %collective-permute-start.18) | collective-permute-done | bytes 852000 | tf_op jit(solution)/shard_map/ppermute | solution.py:45
  93.7 19.7 %collective-permute-done.5 = bf16[64,1664]{1,0:T(8,128)(2,1)S(1)} collective-permute-done((bf16[64,1664]{1,0:T(8,128)(2,1)S(1)}, bf16[64,1664]{1,0:T(8,128)(2,1)S(1)}, u32[]{:S(2)}, u32[]{:S(2)}) %collective-permute-start.5) | collective-permute-done | bytes 213024 | tf_op jit(solution)/shard_map/ppermute | solution.py:54
  113.5 7.9 %collective-permute-done.19 = bf16[64,3328]{1,0:T(8,128)(2,1)S(1)} collective-permute-done((bf16[64,3328]{1,0:T(8,128)(2,1)S(1)}, bf16[64,3328]{1,0:T(8,128)(2,1)S(1)}, u32[]{:S(2)}, u32[]{:S(2)}) %collective-permute-start.19) | collective-permute-done | bytes 426016 | tf_op jit(solution)/shard_map/ppermute | solution.py:45
  125.5 7.9 %collective-permute-done.20 = bf16[64,1664]{1,0:T(8,128)(2,1)S(1)} collective-permute-done((bf16[64,1664]{1,0:T(8,128)(2,1)S(1)}, bf16[64,1664]{1,0:T(8,128)(2,1)S(1)}, u32[]{:S(2)}, u32[]{:S(2)}) %collective-permute-start.20) | collective-permute-done | bytes 213024 | tf_op jit(solution)/shard_map/ppermute | solution.py:54
  133.8 5.4 %collective-permute-done.6 = bf16[128,1664]{1,0:T(8,128)(2,1)S(1)} collective-permute-done((bf16[128,1664]{1,0:T(8,128)(2,1)S(1)}, bf16[128,1664]{1,0:T(8,128)(2,1)S(1)}, u32[]{:S(2)}, u32[]{:S(2)}) %collective-permute-start.6) | collective-permute-done | bytes 426016 | tf_op jit(solution)/shard_map/ppermute | solution.py:54
  139.3 4.2 %convolution_convert_fusion.3 = bf16[256,4096]{1,0:T(8,128)(2,1)S(1)} fusion(bf16[1664,4096]{1,0:T(8,128)(2,1)S(1)} %bitcast.46, bf16[128,1664]{1,0:T(8,128)(2,1)S(1)} %get-tuple-element.31, bf16[128,1664]{1,0:T(8,128)(2,1)S(1)} %get-tuple-element.30), kind=kOutput, calls=%fused_computation.10 | convolution fusion | flops 3492413440 | bytes 16580608 | tf_op jit(solution)/shard_map/dot_general | solution.py:82
  147.5 4.4 %convolution_convert_fusion.2 = bf16[256,4096]{1,0:T(8,128)(2,1)S(1)} fusion(bf16[1664,4096]{1,0:T(8,128)(2,1)S(1)} %bitcast.46, bf16[128,1664]{1,0:T(8,128)(2,1)S(1)} %get-tuple-element.33, bf16[128,1664]{1,0:T(8,128)(2,1)S(1)} %get-tuple-element.32), kind=kOutput, calls=%fused_computation.9 | convolution fusion | flops 3492413440 | bytes 16580608 | tf_op jit(solution)/shard_map/dot_general | solution.py:82
  156.5 5.1 %collective-permute-done.8 = bf16[64,4096]{1,0:T(8,128)(2,1)S(1)} collective-permute-done((bf16[64,4096]{1,0:T(8,128)(2,1)S(1)}, bf16[64,4096]{1,0:T(8,128)(2,1)S(1)}, u32[]{:S(2)}, u32[]{:S(2)}) %collective-permute-start.8) | collective-permute-done | bytes 524320 | tf_op jit(solution)/shard_map/ppermute | solution.py:45
  163.2 6.9 %collective-permute-done.23 = bf16[64,4096]{1,0:T(8,128)(2,1)S(1)} collective-permute-done((bf16[64,4096]{1,0:T(8,128)(2,1)S(1)}, bf16[64,4096]{1,0:T(8,128)(2,1)S(1)}, u32[]{:S(2)}, u32[]{:S(2)}) %collective-permute-start.23) | collective-permute-done | bytes 524320 | tf_op jit(solution)/shard_map/ppermute | solution.py:45
  172.3 4.3 %collective-permute-done.24 = bf16[32,4096]{1,0:T(8,128)(2,1)S(1)} collective-permute-done((bf16[32,4096]{1,0:T(8,128)(2,1)S(1)}, bf16[32,4096]{1,0:T(8,128)(2,1)S(1)}, u32[]{:S(2)}, u32[]{:S(2)}) %collective-permute-start.24) | collective-permute-done | bytes 262176 | tf_op jit(solution)/shard_map/ppermute | solution.py:45
  194.4 5.3 %collective-permute-done.26 = bf16[64,4096]{1,0:T(8,128)(2,1)S(1)} collective-permute-done((bf16[64,4096]{1,0:T(8,128)(2,1)S(1)}, bf16[64,4096]{1,0:T(8,128)(2,1)S(1)}, u32[]{:S(2)}, u32[]{:S(2)}) %collective-permute-start.26) | collective-permute-done | bytes 524320 | tf_op jit(solution)/shard_map/ppermute | solution.py:54
  200.7 14.4 %convolution_convert_fusion.1 = bf16[256,4008]{0,1:T(8,128)(2,1)S(1)} fusion(bf16[4096,4008]{0,1:T(8,128)(2,1)} %param.20, f32[4096]{0:T(1024)S(1)} %copy-done.9, bf16[128,4096]{1,0:T(8,128)(2,1)S(1)} %get-tuple-element.15, bf16[128,4096]{1,0:T(8,128)(2,1)S(1)} %get-tuple-element.14), kind=kOutput, calls=%fused_computation.8 | convolution fusion | flops 8412702720 | bytes 36999168 | tf_op jit(solution)/shard_map/dot_general | solution.py:89
  215.8 14.5 %convolution_convert_fusion = bf16[256,4008]{0,1:T(8,128)(2,1)S(1)} fusion(bf16[4096,4008]{0,1:T(8,128)(2,1)} %param.20, f32[4096]{0:T(1024)S(1)} %copy-done.9, bf16[128,4096]{1,0:T(8,128)(2,1)S(1)} %get-tuple-element.19, bf16[128,4096]{1,0:T(8,128)(2,1)S(1)} %get-tuple-element.18), kind=kOutput, calls=%fused_computation.7 | convolution fusion | flops 8412702720 | bytes 36999168 | tf_op jit(solution)/shard_map/dot_general | solution.py:89
  233.9 6.8 %collective-permute-done.13 = bf16[128,4008]{0,1:T(8,128)(2,1)S(1)} collective-permute-done((bf16[128,4008]{0,1:T(8,128)(2,1)S(1)}, bf16[128,4008]{0,1:T(8,128)(2,1)S(1)}, u32[]{:S(2)}, u32[]{:S(2)}) %collective-permute-start.13) | collective-permute-done | bytes 1026080 | tf_op jit(solution)/shard_map/ppermute | solution.py:45
  244.4 29.3 %collective-permute-done.28 = bf16[128,4008]{0,1:T(8,128)(2,1)} collective-permute-done((bf16[128,4008]{0,1:T(8,128)(2,1)}, bf16[128,4008]{0,1:T(8,128)(2,1)}, u32[]{:S(2)}, u32[]{:S(2)}) %collective-permute-start.28) | collective-permute-done | bytes 1026080 | tf_op jit(solution)/shard_map/ppermute | solution.py:45
  282.0 15.8 %all-reduce = (f32[256]{0:T(256)S(1)}, f32[256]{0:T(256)S(1)}) all-reduce(f32[256]{0:T(256)S(1)} %fusion.3, f32[256]{0:T(256)S(1)} %fusion.1), channel_id=1, replica_groups=mesh['dm'=4,'hv'=8] {'dm'}, use_global_device_ids=true, to_apply=%region_6.7 | all-reduce | flops 512 | bytes 4096 | tf_op jit(solution)/shard_map/psum | solution.py:87
  309.9 8.9 %all-gather = f32[16,3,64]{2,1,0:T(4,128)S(1)} all-gather(f32[2,3,64]{2,1,0:T(4,128)S(1)} %pad_maximum_fusion.20), channel_id=2, replica_groups=mesh['dm'=4,'hv'=8] {'hv'}, dimensions={0}, use_global_device_ids=true | all-gather | bytes 13824 | tf_op jit(solution)/shard_map/all_gather | solution.py:99
  319.0 16.3 %all-gather.2 = f32[4,2,64]{2,1,0:T(2,128)S(1)} all-gather(f32[1,2,64]{2,1,0:T(2,128)S(1)} %subtract_bitcast_fusion), channel_id=3, replica_groups=mesh['dm'=4,'hv'=8] {'dm'}, dimensions={0}, use_global_device_ids=true | all-gather | bytes 2560 | tf_op jit(solution)/shard_map/all_gather | solution.py:103
  (171 shorter events, 95.9 us)
Async XLA Ops:
  10.1 9.2 %collective-permute-start.15 = (bf16[32,4096]{1,0:T(8,128)(2,1)S(1)}, bf16[32,4096]{1,0:T(8,128)(2,1)S(1)}, u32[]{:S(2)}, u32[]{:S(2)}) collective-permute-start(bf16[32,4096]{1,0:T(8,128)(2,1)S(1)} %get-tuple-element.42), channel_id=1, source_target_pairs={{0,4},{1,3},{2,6},{3,1},{4,0},{5,7},{6,2},{7,5},{8,12},{9,11},{10,... | collective-permute-start | bytes 786440 | tf_op jit(solution)/shard_map/ppermute | solution.py:54
  12.3 9.3 %collective-permute-start.1 = (bf16[64,4096]{1,0:T(8,128)(2,1)S(1)}, bf16[64,4096]{1,0:T(8,128)(2,1)S(1)}, u32[]{:S(2)}, u32[]{:S(2)}) collective-permute-start(bf16[64,4096]{1,0:T(8,128)(2,1)S(1)} %pad_maximum_fusion.14), channel_id=1, source_target_pairs={{0,2},{1,5},{2,0},{3,7},{4,6},{5,1},{6,4},{7,3},{8,10},{9,13},{10,... | collective-permute-start | bytes 1572872 | tf_op jit(solution)/shard_map/ppermute | solution.py:54
  19.5 9.3 %collective-permute-start.16 = (bf16[64,4096]{1,0:T(8,128)(2,1)S(1)}, bf16[64,4096]{1,0:T(8,128)(2,1)S(1)}, u32[]{:S(2)}, u32[]{:S(2)}) collective-permute-start(bf16[64,4096]{1,0:T(8,128)(2,1)S(1)} %pad_maximum_fusion.16), channel_id=1, source_target_pairs={{0,2},{1,5},{2,0},{3,7},{4,6},{5,1},{6,4},{7,3},{8,10},{9,13},{10,... | collective-permute-start | bytes 1572872 | tf_op jit(solution)/shard_map/ppermute | solution.py:54
  29.1 14.1 %collective-permute-start.17 = (bf16[128,4096]{1,0:T(8,128)(2,1)S(1)}, bf16[128,4096]{1,0:T(8,128)(2,1)S(1)}, u32[]{:S(2)}, u32[]{:S(2)}) collective-permute-start(bf16[128,4096]{1,0:T(8,128)(2,1)S(1)} %pad_maximum_fusion.12), channel_id=1, source_target_pairs={{0,1},{1,0},{2,3},{3,2},{4,5},{5,4},{6,7},{7,6},{8,9},{9,8},{10,11... | collective-permute-start | bytes 3145736 | tf_op jit(solution)/shard_map/ppermute | solution.py:54
  41.1 21.9 %collective-permute-start.3 = (bf16[128,3328]{1,0:T(8,128)(2,1)S(1)}, bf16[128,3328]{1,0:T(8,128)(2,1)S(1)}, u32[]{:S(2)}, u32[]{:S(2)}) collective-permute-start(bf16[128,3328]{1,0:T(8,128)(2,1)S(1)} %fusion.13), channel_id=1, source_target_pairs={{0,8},{8,0},{16,24},{24,16},{1,9},{9,1},{17,25},{25,17},{2,10},{10... | collective-permute-start | bytes 2555912 | tf_op jit(solution)/shard_map/ppermute | solution.py:45
  55.1 35.1 %collective-permute-start.18 = (bf16[128,3328]{1,0:T(8,128)(2,1)S(1)}, bf16[128,3328]{1,0:T(8,128)(2,1)S(1)}, u32[]{:S(2)}, u32[]{:S(2)}) collective-permute-start(bf16[128,3328]{1,0:T(8,128)(2,1)S(1)} %fusion.11), channel_id=1, source_target_pairs={{0,8},{8,0},{16,24},{24,16},{1,9},{9,1},{17,25},{25,17},{2,10},{10... | collective-permute-start | bytes 2555912 | tf_op jit(solution)/shard_map/ppermute | solution.py:45
  63.2 27.1 %collective-permute-start.4 = (bf16[64,3328]{1,0:T(8,128)(2,1)S(1)}, bf16[64,3328]{1,0:T(8,128)(2,1)S(1)}, u32[]{:S(2)}, u32[]{:S(2)}) collective-permute-start(bf16[64,3328]{1,0:T(8,128)(2,1)S(1)} %constant_dynamic-slice_fusion.11), channel_id=1, source_target_pairs={{0,16},{8,24},{16,0},{24,8},{1,17},{9,25},{17,1},{25,9},{2,18},{10... | collective-permute-start | bytes 1277960 | tf_op jit(solution)/shard_map/ppermute | solution.py:45
  90.6 22.8 %collective-permute-start.5 = (bf16[64,1664]{1,0:T(8,128)(2,1)S(1)}, bf16[64,1664]{1,0:T(8,128)(2,1)S(1)}, u32[]{:S(2)}, u32[]{:S(2)}) collective-permute-start(bf16[64,1664]{1,0:T(8,128)(2,1)S(1)} %fusion.24), channel_id=1, source_target_pairs={{0,16},{8,24},{16,0},{24,8},{1,17},{9,25},{17,1},{25,9},{2,18},{10... | collective-permute-start | bytes 638984 | tf_op jit(solution)/shard_map/ppermute | solution.py:54
  93.1 28.3 %collective-permute-start.19 = (bf16[64,3328]{1,0:T(8,128)(2,1)S(1)}, bf16[64,3328]{1,0:T(8,128)(2,1)S(1)}, u32[]{:S(2)}, u32[]{:S(2)}) collective-permute-start(bf16[64,3328]{1,0:T(8,128)(2,1)S(1)} %constant_dynamic-slice_fusion.5), channel_id=1, source_target_pairs={{0,16},{8,24},{16,0},{24,8},{1,17},{9,25},{17,1},{25,9},{2,18},{10... | collective-permute-start | bytes 1277960 | tf_op jit(solution)/shard_map/ppermute | solution.py:45
  121.7 11.8 %collective-permute-start.20 = (bf16[64,1664]{1,0:T(8,128)(2,1)S(1)}, bf16[64,1664]{1,0:T(8,128)(2,1)S(1)}, u32[]{:S(2)}, u32[]{:S(2)}) collective-permute-start(bf16[64,1664]{1,0:T(8,128)(2,1)S(1)} %fusion.23), channel_id=1, source_target_pairs={{0,16},{8,24},{16,0},{24,8},{1,17},{9,25},{17,1},{25,9},{2,18},{10... | collective-permute-start | bytes 638984 | tf_op jit(solution)/shard_map/ppermute | solution.py:54
  121.8 17.4 %collective-permute-start.6 = (bf16[128,1664]{1,0:T(8,128)(2,1)S(1)}, bf16[128,1664]{1,0:T(8,128)(2,1)S(1)}, u32[]{:S(2)}, u32[]{:S(2)}) collective-permute-start(bf16[128,1664]{1,0:T(8,128)(2,1)S(1)} %pad_maximum_fusion.18), channel_id=1, source_target_pairs={{0,8},{8,0},{16,24},{24,16},{1,9},{9,1},{17,25},{25,17},{2,10},{10... | collective-permute-start | bytes 1277960 | tf_op jit(solution)/shard_map/ppermute | solution.py:54
  133.7 13.7 %collective-permute-start.21 = (bf16[128,1664]{1,0:T(8,128)(2,1)S(1)}, bf16[128,1664]{1,0:T(8,128)(2,1)S(1)}, u32[]{:S(2)}, u32[]{:S(2)}) collective-permute-start(bf16[128,1664]{1,0:T(8,128)(2,1)S(1)} %pad_maximum_fusion.19), channel_id=1, source_target_pairs={{0,8},{8,0},{16,24},{24,16},{1,9},{9,1},{17,25},{25,17},{2,10},{10... | collective-permute-start | bytes 1277960 | tf_op jit(solution)/shard_map/ppermute | solution.py:54
  143.6 8.4 %collective-permute-start.7 = (bf16[128,4096]{1,0:T(8,128)(2,1)S(1)}, bf16[128,4096]{1,0:T(8,128)(2,1)S(1)}, u32[]{:S(2)}, u32[]{:S(2)}) collective-permute-start(bf16[128,4096]{1,0:T(8,128)(2,1)S(1)} %constant_dynamic-slice_fusion.10), channel_id=1, source_target_pairs={{0,1},{1,0},{2,3},{3,2},{4,5},{5,4},{6,7},{7,6},{8,9},{9,8},{10,11... | collective-permute-start | bytes 3145736 | tf_op jit(solution)/shard_map/ppermute | solution.py:45
  152.4 9.2 %collective-permute-start.8 = (bf16[64,4096]{1,0:T(8,128)(2,1)S(1)}, bf16[64,4096]{1,0:T(8,128)(2,1)S(1)}, u32[]{:S(2)}, u32[]{:S(2)}) collective-permute-start(bf16[64,4096]{1,0:T(8,128)(2,1)S(1)} %constant_dynamic-slice_fusion.9), channel_id=1, source_target_pairs={{0,2},{1,5},{2,0},{3,7},{4,6},{5,1},{6,4},{7,3},{8,10},{9,13},{10,... | collective-permute-start | bytes 1572872 | tf_op jit(solution)/shard_map/ppermute | solution.py:45
  155.0 15.0 %collective-permute-start.23 = (bf16[64,4096]{1,0:T(8,128)(2,1)S(1)}, bf16[64,4096]{1,0:T(8,128)(2,1)S(1)}, u32[]{:S(2)}, u32[]{:S(2)}) collective-permute-start(bf16[64,4096]{1,0:T(8,128)(2,1)S(1)} %constant_dynamic-slice_fusion.3), channel_id=1, source_target_pairs={{0,2},{1,5},{2,0},{3,7},{4,6},{5,1},{6,4},{7,3},{8,10},{9,13},{10,... | collective-permute-start | bytes 1572872 | tf_op jit(solution)/shard_map/ppermute | solution.py:45
  161.8 10.5 %collective-permute-start.9 = (bf16[32,4096]{1,0:T(8,128)(2,1)S(1)}, bf16[32,4096]{1,0:T(8,128)(2,1)S(1)}, u32[]{:S(2)}, u32[]{:S(2)}) collective-permute-start(bf16[32,4096]{1,0:T(8,128)(2,1)S(1)} %constant_dynamic-slice_fusion.8), channel_id=1, source_target_pairs={{0,4},{1,3},{2,6},{3,1},{4,0},{5,7},{6,2},{7,5},{8,12},{9,11},{10,... | collective-permute-start | bytes 786440 | tf_op jit(solution)/shard_map/ppermute | solution.py:45
  180.1 10.3 %collective-permute-start.25 = (bf16[32,4096]{1,0:T(8,128)(2,1)S(1)}, bf16[32,4096]{1,0:T(8,128)(2,1)S(1)}, u32[]{:S(2)}, u32[]{:S(2)}) collective-permute-start(bf16[32,4096]{1,0:T(8,128)(2,1)S(1)} %get-tuple-element.41), channel_id=1, source_target_pairs={{0,4},{1,3},{2,6},{3,1},{4,0},{5,7},{6,2},{7,5},{8,12},{9,11},{10,... | collective-permute-start | bytes 786440 | tf_op jit(solution)/shard_map/ppermute | solution.py:54
  184.8 9.2 %collective-permute-start.11 = (bf16[64,4096]{1,0:T(8,128)(2,1)S(1)}, bf16[64,4096]{1,0:T(8,128)(2,1)S(1)}, u32[]{:S(2)}, u32[]{:S(2)}) collective-permute-start(bf16[64,4096]{1,0:T(8,128)(2,1)S(1)} %pad_maximum_fusion.15), channel_id=1, source_target_pairs={{0,2},{1,5},{2,0},{3,7},{4,6},{5,1},{6,4},{7,3},{8,10},{9,13},{10,... | collective-permute-start | bytes 1572872 | tf_op jit(solution)/shard_map/ppermute | solution.py:54
  190.4 9.2 %collective-permute-start.26 = (bf16[64,4096]{1,0:T(8,128)(2,1)S(1)}, bf16[64,4096]{1,0:T(8,128)(2,1)S(1)}, u32[]{:S(2)}, u32[]{:S(2)}) collective-permute-start(bf16[64,4096]{1,0:T(8,128)(2,1)S(1)} %pad_maximum_fusion.17), channel_id=1, source_target_pairs={{0,2},{1,5},{2,0},{3,7},{4,6},{5,1},{6,4},{7,3},{8,10},{9,13},{10,... | collective-permute-start | bytes 1572872 | tf_op jit(solution)/shard_map/ppermute | solution.py:54
  200.0 15.3 %collective-permute-start.27 = (bf16[128,4096]{1,0:T(8,128)(2,1)S(1)}, bf16[128,4096]{1,0:T(8,128)(2,1)S(1)}, u32[]{:S(2)}, u32[]{:S(2)}) collective-permute-start(bf16[128,4096]{1,0:T(8,128)(2,1)S(1)} %pad_maximum_fusion.13), channel_id=1, source_target_pairs={{0,1},{1,0},{2,3},{3,2},{4,5},{5,4},{6,7},{7,6},{8,9},{9,8},{10,11... | collective-permute-start | bytes 3145736 | tf_op jit(solution)/shard_map/ppermute | solution.py:54
  215.2 25.5 %collective-permute-start.13 = (bf16[128,4008]{0,1:T(8,128)(2,1)S(1)}, bf16[128,4008]{0,1:T(8,128)(2,1)S(1)}, u32[]{:S(2)}, u32[]{:S(2)}) collective-permute-start(bf16[128,4008]{0,1:T(8,128)(2,1)S(1)} %constant_dynamic-slice_fusion.7), channel_id=1, source_target_pairs={{0,8},{8,0},{16,24},{24,16},{1,9},{9,1},{17,25},{25,17},{2,10},{10... | collective-permute-start | bytes 3078152 | tf_op jit(solution)/shard_map/ppermute | solution.py:45
  231.4 42.3 %collective-permute-start.28 = (bf16[128,4008]{0,1:T(8,128)(2,1)}, bf16[128,4008]{0,1:T(8,128)(2,1)}, u32[]{:S(2)}, u32[]{:S(2)}) collective-permute-start(bf16[128,4008]{0,1:T(8,128)(2,1)} %constant_dynamic-slice_fusion.1), channel_id=1, source_target_pairs={{0,8},{8,0},{16,24},{24,16},{1,9},{9,1},{17,25},{25,17},{2,10},{10... | collective-permute-start | bytes 3078152 | tf_op jit(solution)/shard_map/ppermute | solution.py:45
  242.6 55.4 %collective-permute-start.14 = (bf16[64,4008]{1,0:T(8,128)(2,1)}, bf16[64,4008]{1,0:T(8,128)(2,1)}, u32[]{:S(2)}, u32[]{:S(2)}) collective-permute-start(bf16[64,4008]{1,0:T(8,128)(2,1)} %copy.23), channel_id=1, source_target_pairs={{0,16},{8,24},{16,0},{24,8},{1,17},{9,25},{17,1},{25,9},{2,18},{10... | collective-permute-start | bytes 1539080 | tf_op jit(solution)/shard_map/ppermute | solution.py:45
  279.2 26.2 %collective-permute-start.29 = (bf16[64,4008]{1,0:T(8,128)(2,1)}, bf16[64,4008]{1,0:T(8,128)(2,1)}, u32[]{:S(2)}, u32[]{:S(2)}) collective-permute-start(bf16[64,4008]{1,0:T(8,128)(2,1)} %copy.25), channel_id=1, source_target_pairs={{0,16},{8,24},{16,0},{24,8},{1,17},{9,25},{17,1},{25,9},{2,18},{10... | collective-permute-start | bytes 1539080 | tf_op jit(solution)/shard_map/ppermute | solution.py:45
  (20 other events, 529.6 us)
